TPU v7x, 32 devices: a whole 2x2x4 slice. The times are simulated.
32 devices in a mesh: ctx: 8 (over z, y), tp: 4 (over x, core).
Axes of the slice: x: 2, y: 2, z: 4, core: 2. Of those that a mesh axis runs over, the one named last changes fastest.
Arguments:
- query_one: bfloat16 [2048, 8192], P('ctx', 'tp'), may hold values from -6 to 6
- key_one: bfloat16 [2048, 8192], P('ctx', 'tp'), may hold values from -6 to 6
- value_one: bfloat16 [2048, 8192], P('ctx', 'tp'), may hold values from -6 to 6
- residual_in: bfloat16 [2048, 8192], P('ctx', 'tp'), may hold values from -50 to 50
- medium_taps: bfloat16 [128, 8192], P(None, 'tp'), may hold values from -0.5 to 0.5
- skip_one: float32 [8192], P('tp'), may hold values from -4 to 4
- norm_gain: float32 [8192], P('tp'), may hold values from 0.5 to 1.5
- query_two: bfloat16 [2048, 8192], P('ctx', 'tp'), may hold values from -6 to 6
- key_two: bfloat16 [2048, 8192], P('ctx', 'tp'), may hold values from -6 to 6
- residues: float32 [16, 8192], P(None, 'tp'), may hold values from -2 to 2
- decay_rates: float32 [16, 8192], P(None, 'tp'), may hold values from 0.00048828125 to 0.03
- skip_two: float32 [8192], P('tp'), may hold values from -4 to 4
Outputs:
- residual_out: bfloat16 [2048, 8192], P('ctx', 'tp')
- long_output: bfloat16 [2048, 8192], P('ctx', 'tp')
All inputs are finite; a program needn't handle non-finite values.
Results may differ from a plain program's by a relative error of at most 0.013.
Values may be sent and summed in bfloat16 or wider, within the bound.
A program may use at most 128 MiB of HBM per device.

v0:
```python
import functools

import jax
import jax.numpy as jnp
import ml_dtypes
import numpy as np
from jax import lax
from jax.experimental import pallas as pl
from jax.experimental.pallas import tpu as pltpu
from jax.sharding import PartitionSpec as P

F32 = jnp.float32
BF16 = jnp.bfloat16
MESH = pl.DeviceIdType.MESH
LANES = 128
CHUNK = 512


def half_bin_tables(period, rows_in, out_from, out_to):
    bins = np.arange(period // 2)[:, None] + 0.5
    angle = 2.0 * np.pi / period * bins * np.arange(period)[None, :]
    forward = np.concatenate([np.cos(angle), -np.sin(angle)], axis=0)[:, :rows_in]
    inverse = np.concatenate([np.cos(angle), -np.sin(angle)], axis=0).T[out_from:out_to] * (2.0 / period)
    return [x.astype(ml_dtypes.bfloat16).astype(np.float32) for x in (forward, inverse)]


def dot(left, right):
    return jnp.dot(left, right, preferred_element_type=F32)


def complex_product(x, h):
    half = x.shape[0] // 2
    xr, xi, hr, hi = x[:half], x[half:], h[:half], h[half:]
    return jnp.concatenate([xr * hr - xi * hi, xr * hi + xi * hr], axis=0).astype(BF16)


def kernel(
    n, tp_n,
    q1_h, k1_h, v1_h, res_h, taps_h, skip1, gain, q2_h, k2_h, residues, rates, skip2,
    fm_h, gm_h, fl_h, gl_h,
    rout_h, lout_h,
    q1, k1, v1, res, taps, q2, k2, fm32, gm32, fl32, gl32, fm, gm, fl, gl,
    buf, spec_m, spec_l, hbuf, rout, v2, loc, obuf,
    sq_acc, sq_send, sq_recv, scale, state, carry, st_send, st_recv,
    in_sem, out_sem, halo_send, halo_recv, sq_ssem, sq_rsem, st_ssem, st_rsem,
):
    T, C = q1.shape
    K = taps.shape[0]
    M = residues.shape[0]
    groups = C // LANES
    chunks = C // CHUNK
    steps = (n - 1).bit_length()
    d = lax.axis_index("ctx")
    t = lax.axis_index("tp")

    def lane(g):
        return pl.ds(pl.multiple_of(g * LANES, LANES), LANES)

    def cols(j):
        return pl.ds(pl.multiple_of(j * CHUNK, CHUNK), CHUNK)

    pairs = [
        (k1_h, k1), (v1_h, v1), (fm_h, fm32), (taps_h, taps), (gm_h, gm32), (q1_h, q1), (res_h, res),
        (fl_h, fl32), (k2_h, k2), (gl_h, gl32), (q2_h, q2),
    ]
    loads = [pltpu.make_async_copy(a, b, in_sem.at[i]) for i, (a, b) in enumerate(pairs)]
    for load in loads:
        load.start()

    barrier = pltpu.get_barrier_semaphore()
    shifts = [1 << i for i in range(steps)]
    for s in shifts:
        @pl.when(d + s < n)
        def _(s=s):
            pl.semaphore_signal(barrier, inc=1, device_id=(d + s, t), device_id_type=MESH)

        @pl.when(d >= s)
        def _(s=s):
            pl.semaphore_signal(barrier, inc=1, device_id=(d - s, t), device_id_type=MESH)
    for o in range(1, tp_n):
        pl.semaphore_signal(barrier, inc=1, device_id=(d, lax.rem(t + o, tp_n)), device_id_type=MESH)
    peers = tp_n - 1
    for s in shifts:
        peers = peers + (d + s < n).astype(jnp.int32) + (d >= s).astype(jnp.int32)
    pl.semaphore_wait(barrier, peers)

    def halo(j):
        c = pl.ds(j * CHUNK, CHUNK)
        return pltpu.make_async_remote_copy(
            src_ref=buf.at[pl.ds(T, K), c], dst_ref=buf.at[pl.ds(0, K), c],
            send_sem=halo_send.at[j], recv_sem=halo_recv.at[j],
            device_id=(lax.rem(d + 1, n), t), device_id_type=MESH)

    def product(row, j):
        c = pl.ds(j * CHUNK, CHUNK)
        r = pl.ds(row, K)
        buf[pl.ds(K + row, K), c] = (k1[r, c].astype(F32) * v1[r, c].astype(F32)).astype(BF16)

    loads[0].wait()
    loads[1].wait()
    for j in range(chunks):
        product(T - K, j)

        @pl.when(d + 1 < n)
        def _(j=j):
            halo(j).start()
    for j in range(chunks):
        product(0, j)

    @pl.when(d == 0)
    def _():
        buf[pl.ds(0, K), :] = jnp.zeros((K, C), BF16)

    for i in range(2, 7):
        loads[i].wait()
    fm[...] = fm32[...].astype(BF16)
    gm[...] = gm32[...].astype(BF16)

    def medium(row, j):
        c = cols(j)
        r = pl.ds(row, K)
        x = dot(fm[...], buf[pl.ds(row, 2 * K), c])
        filtered = dot(gm[...], complex_product(x, spec_m[:, c]))
        mixed = filtered + skip1[:, c] * buf[pl.ds(K + row, K), c].astype(F32)
        out = (res[r, c].astype(F32) + q1[r, c].astype(F32) * mixed).astype(BF16)
        rout[r, c] = out
        wide = out.astype(F32)
        square = wide * wide
        total = sq_acc[...]
        for i in range(CHUNK // LANES):
            total = total + square[:, i * LANES:(i + 1) * LANES]
        sq_acc[...] = total

    def send_squares(half):
        summed = jnp.sum(sq_acc[...], axis=1, keepdims=True)
        sq_send[half] = jnp.broadcast_to(summed, (K, LANES)).T[:8]
        for o in range(1, tp_n):
            squares(half, o).start()

    def squares(half, o):
        return pltpu.make_async_remote_copy(
            src_ref=sq_send.at[half], dst_ref=sq_recv.at[half, o - 1],
            send_sem=sq_ssem.at[half, o - 1], recv_sem=sq_rsem.at[half, o - 1],
            device_id=(d, lax.rem(t + o, tp_n)), device_id_type=MESH)

    def take_squares(half):
        total = sq_send[half]
        for o in range(1, tp_n):
            squares(half, o).wait()
            total = total + sq_recv[half, o - 1]
        root = lax.rsqrt(total * (1.0 / (C * tp_n)) + 1e-05)
        scale[...] = jnp.concatenate([root] * (K // 8), axis=0).T

    def mode_rows(g, offset, sign):
        sub = lax.broadcasted_iota(jnp.int32, (8, LANES), 0).astype(F32) * sign + offset
        eight, first = [], []
        for m in range(M):
            rate = jnp.broadcast_to(rates[pl.ds(m, 1), lane(g)], (8, LANES))
            eight.append(jnp.exp(rate * -8.0))
            first.append(jnp.exp(-rate * sub))
        return eight, first

    def weight(g, m):
        rate = rates[pl.ds(m, 1), lane(g)]
        return residues[pl.ds(m, 1), lane(g)] * jnp.sqrt(rate)

    def tree_sum(terms):
        while len(terms) > 1:
            terms = [a + b for a, b in zip(terms[::2], terms[1::2])] + terms[len(terms) // 2 * 2:]
        return terms[0]

    def next_rows(terms, eight):
        top = tree_sum(terms)
        terms = [p * a for p, a in zip(terms, eight)]
        bottom = tree_sum(terms)
        return jnp.concatenate([top, bottom], axis=0), [p * a for p, a in zip(terms, eight)]

    def normed(half, g, _):
        c = lane(g)
        eight, first = mode_rows(g, 7.0, -1.0)
        held = [jnp.zeros((8, LANES), F32)] * M
        for i in range(K // 16):
            r = pl.ds(half * K + i * 16, 16)
            value = (k2[r, c].astype(F32) * rout[r, c].astype(F32) * scale[pl.ds(i * 16, 16), :] * gain[:, c]).astype(BF16)
            v2[r, c] = value
            wide = value.astype(F32)
            held = [h * a + wide[:8] for h, a in zip(held, eight)]
            held = [h * a + wide[8:] for h, a in zip(held, eight)]
        for m in range(M):
            part = jnp.sum(held[m] * first[m], axis=0, keepdims=True)
            row = pl.ds(m, 1)
            if half == 0:
                state[row, c] = state[row, c] + jnp.exp(rates[row, c] * -float(K)) * part
            else:
                state[row, c] = part
        return 0

    def medium_spectrum(j, _):
        c = cols(j)
        spec_m[:, c] = dot(fm[:, :K], taps[:, c])
        medium(K, j)
        return 0

    sq_acc[...] = jnp.zeros_like(sq_acc)
    lax.fori_loop(0, chunks, medium_spectrum, 0)
    send_squares(1)

    def long_taps(g, _):
        eight, first = mode_rows(g, 0.0, 1.0)
        terms = [first[m] * weight(g, m) for m in range(M)]
        for i in range(T // 16):
            rows, terms = next_rows(terms, eight)
            hbuf[pl.ds(i * 16, 16), lane(g)] = rows.astype(BF16)
        return 0

    lax.fori_loop(0, groups, long_taps, 0)
    loads[7].wait()
    fl[...] = fl32[...].astype(BF16)

    def long_spectrum(j, _):
        spec_l[:, cols(j)] = dot(fl[...], hbuf[:, cols(j)])
        return 0

    lax.fori_loop(0, chunks, long_spectrum, 0)
    loads[8].wait()
    take_squares(1)
    lax.fori_loop(0, groups, functools.partial(normed, 1), 0)

    sq_acc[...] = jnp.zeros_like(sq_acc)
    for j in range(chunks):
        @pl.when(d >= 1)
        def _(j=j):
            halo(j).wait_recv()
        medium(0, j)
    send_squares(0)
    rout_copy = pltpu.make_async_copy(rout, rout_h, out_sem.at[chunks])
    rout_copy.start()
    take_squares(0)
    lax.fori_loop(0, groups, functools.partial(normed, 0), 0)
    loads[9].wait()
    gl[...] = gl32[...].astype(BF16)
    loads[10].wait()

    def hop(i):
        return pltpu.make_async_remote_copy(
            src_ref=st_send.at[i], dst_ref=st_recv.at[i],
            send_sem=st_ssem.at[i], recv_sem=st_rsem.at[i],
            device_id=(lax.rem(d + shifts[i], n), t), device_id_type=MESH)

    def inside(j, _):
        c = cols(j)
        y = complex_product(dot(fl[...], v2[:, c]), spec_l[:, c])
        loc[:, c] = dot(gl[...], y) + skip2[:, c] * v2[:, c].astype(F32)
        return 0

    carry[...] = jnp.zeros_like(carry)
    done = 0
    for i, s in enumerate(shifts):
        st_send[i] = state[...].astype(BF16)

        @pl.when(d + s < n)
        def _(i=i):
            hop(i).start()
        upto = chunks * (i + 1) // steps
        lax.fori_loop(done, upto, inside, 0)
        done = upto

        @pl.when(d >= s)
        def _(i=i, s=s):
            hop(i).wait_recv()
            arrived = st_recv[i].astype(F32)
            rate = rates[...]
            carry[...] += jnp.exp(rate * -float(T * (s - 1))) * arrived
            state[...] += jnp.exp(rate * -float(T * s)) * arrived

    def finish(g, _):
        c = lane(g)
        eight, first = mode_rows(g, 1.0, 1.0)
        terms = [first[m] * (weight(g, m) * carry[pl.ds(m, 1), c]) for m in range(M)]
        for i in range(T // 16):
            r = pl.ds(i * 16, 16)
            rows, terms = next_rows(terms, eight)
            obuf[r, c] = (q2[r, c].astype(F32) * (loc[r, c] + rows)).astype(BF16)
        return 0

    out_copies = []
    per = groups // chunks
    for j in range(chunks):
        lax.fori_loop(j * per, (j + 1) * per, finish, 0)
        c = pl.ds(j * CHUNK, CHUNK)
        copy = pltpu.make_async_copy(obuf.at[:, c], lout_h.at[:, c], out_sem.at[j])
        copy.start()
        out_copies.append(copy)

    for j in range(chunks):
        @pl.when(d + 1 < n)
        def _(j=j):
            halo(j).wait_send()
    for i, s in enumerate(shifts):
        @pl.when(d + s < n)
        def _(i=i):
            hop(i).wait_send()
    rout_copy.wait()
    for copy in out_copies:
        copy.wait()


def on_device(n, tp_n, q1, k1, v1, res, taps, skip1, gain, q2, k2, residues, rates, skip2):
    T, C = q1.shape
    K = taps.shape[0]
    M = residues.shape[0]
    assert T == 2 * K and C % CHUNK == 0
    chunks = C // CHUNK
    steps = (n - 1).bit_length()
    fm, gm = half_bin_tables(2 * K, 2 * K, K, 2 * K)
    fl, gl = half_bin_tables(2 * T, T, 0, T)
    hbm = pl.BlockSpec(memory_space=pl.ANY)
    vmem = pl.BlockSpec(memory_space=pltpu.VMEM)
    wide = pltpu.VMEM((T, C), BF16)
    return pl.pallas_call(
        functools.partial(kernel, n, tp_n),
        out_shape=[jax.ShapeDtypeStruct((T, C), BF16)] * 2,
        in_specs=[hbm] * 5 + [vmem] * 2 + [hbm] * 2 + [vmem] * 3 + [hbm] * 4,
        out_specs=[hbm] * 2,
        scratch_shapes=[
            wide, wide, wide, wide, pltpu.VMEM((K, C), BF16), wide, wide,
            pltpu.VMEM(fm.shape, F32), pltpu.VMEM(gm.shape, F32),
            pltpu.VMEM(fl.shape, F32), pltpu.VMEM(gl.shape, F32),
            pltpu.VMEM(fm.shape, BF16), pltpu.VMEM(gm.shape, BF16),
            pltpu.VMEM(fl.shape, BF16), pltpu.VMEM(gl.shape, BF16),
            pltpu.VMEM((T + K, C), BF16),
            pltpu.VMEM((2 * K, C), F32),
            pltpu.VMEM((2 * T, C), F32),
            wide, wide, wide,
            pltpu.VMEM((T, C), F32),
            wide,
            pltpu.VMEM((K, LANES), F32),
            pltpu.VMEM((2, 8, K), F32),
            pltpu.VMEM((2, tp_n - 1, 8, K), F32),
            pltpu.VMEM((K, LANES), F32),
            pltpu.VMEM((M, C), F32),
            pltpu.VMEM((M, C), F32),
            pltpu.VMEM((steps, M, C), BF16),
            pltpu.VMEM((steps, M, C), BF16),
            pltpu.SemaphoreType.DMA((11,)),
            pltpu.SemaphoreType.DMA((chunks + 1,)),
            pltpu.SemaphoreType.DMA((chunks,)),
            pltpu.SemaphoreType.DMA((chunks,)),
            pltpu.SemaphoreType.DMA((2, tp_n - 1)),
            pltpu.SemaphoreType.DMA((2, tp_n - 1)),
            pltpu.SemaphoreType.DMA((steps,)),
            pltpu.SemaphoreType.DMA((steps,)),
        ],
        compiler_params=pltpu.CompilerParams(
            collective_id=0, has_side_effects=True, vmem_limit_bytes=56 * 2**20),
        cost_estimate=pl.CostEstimate(
            flops=2 * 620000 * C, bytes_accessed=10 * T * C * 2, transcendentals=M * C * 16),
    )(q1, k1, v1, res, taps, skip1.reshape(1, C), gain.reshape(1, C), q2, k2, residues, rates,
      skip2.reshape(1, C), jnp.asarray(fm), jnp.asarray(gm), jnp.asarray(fl), jnp.asarray(gl))


def solution(mesh):
    rows = P("ctx", "tp")
    in_specs = (
        rows, rows, rows, rows, P(None, "tp"), P("tp"), P("tp"), rows, rows,
        P(None, "tp"), P(None, "tp"), P("tp"),
    )
    return jax.shard_map(
        functools.partial(on_device, mesh.shape["ctx"], mesh.shape["tp"]),
        mesh=mesh, in_specs=in_specs, out_specs=(rows, rows), check_vma=False)
```

profile of v0, /device:TPU:20, one launch (start us, length us, event | category | flops | bytes accessed | tf_op | source)
XLA Modules:
  0.0 38.6 jit_solution(17274556734588709798)
XLA Ops:
  0.6 34.6 %shard_map.167 = (bf16[256,2048]{1,0:T(8,128)(2,1)}, bf16[256,2048]{1,0:T(8,128)(2,1)}) custom-call(bf16[256,2048]{1,0:T(8,128)(2,1)} %q1_h.1, bf16[256,2048]{1,0:T(8,128)(2,1)} %k1_h.1, bf16[256,2048]{1,0:T(8,128)(2,1)} %v1_h.1, bf16[256,2048]{1,0:T(8,128)(2,1)} %res_h.1, bf16[128,2048]{1,0:T(8,128)(2,1)} %taps_h.1, f32[1,2048]{1,0:T(1,128)} %bitcast.3, ...), custom_call_target="tpu_custom_call" | custom-call | flops 2539520000 | bytes 10485760 | tf_op jit(solution)/shard_map/pallas_call | solution.py:320
  35.3 0.0 copy-start
  35.3 2.4 %copy.20 = bf16[256,2048]{1,0:T(8,128)(2,1)} copy(bf16[256,2048]{1,0:T(8,128)(2,1)} %get-tuple-element.4) | data formatting | bytes 2097152
  37.7 0.0 copy-done
  37.7 1.0 %copy.21 = bf16[256,2048]{1,0:T(8,128)(2,1)} copy(bf16[256,2048]{1,0:T(8,128)(2,1)S(1)} %copy-done) | data formatting | bytes 2097152
Async XLA Ops:
  35.3 2.4 %copy-start = (bf16[256,2048]{1,0:T(8,128)(2,1)S(1)}, bf16[256,2048]{1,0:T(8,128)(2,1)}, u32[]{:S(2)}) copy-start(bf16[256,2048]{1,0:T(8,128)(2,1)} %get-tuple-element.5) | copy-start | bytes 3145732
where the time goes:
time: 38.8 us; the launch traced here: 38.6 us
  Pallas kernels  34.6 us (89%)
  local copies, waits for them, and re-layouts  3.37 us (9%)
  between operations  0.65 us (2%)
    pallas_call x1, Pallas kernels, on_device(): pl.pallas_call(functools.partial(kernel, n, tp_n), out_shape=[jax.ShapeDt...  34.6 us
    unnamed x4, local copies, waits for them, and re-layouts  3.37 us

commit v1 on v0

--- a/solution.py
+++ b/solution.py
@@ -41,7 +41,7 @@
     rout_h, lout_h,
     q1, k1, v1, res, taps, q2, k2, fm32, gm32, fl32, gl32, fm, gm, fl, gl,
     buf, spec_m, spec_l, hbuf, rout, v2, loc, obuf,
-    sq_acc, sq_send, sq_recv, scale, state, carry, st_send, st_recv,
+    sq_acc, sq_send, sq_recv, scale, eight_t, weight_t, up_t, down_t, low, state, carry, st_send, st_recv,
     in_sem, out_sem, halo_send, halo_recv, sq_ssem, sq_rsem, st_ssem, st_rsem,
 ):
     T, C = q1.shape
@@ -79,28 +79,27 @@
             pl.semaphore_signal(barrier, inc=1, device_id=(d - s, t), device_id_type=MESH)
     for o in range(1, tp_n):
         pl.semaphore_signal(barrier, inc=1, device_id=(d, lax.rem(t + o, tp_n)), device_id_type=MESH)
+    def halo(j):
+        c = pl.ds(j * CHUNK, CHUNK)
+        return pltpu.make_async_remote_copy(
+            src_ref=buf.at[pl.ds(T, K), c], dst_ref=buf.at[pl.ds(0, K), c],
+            send_sem=halo_send.at[j], recv_sem=halo_recv.at[j],
+            device_id=(lax.rem(d + 1, n), t), device_id_type=MESH)
+
+    def product(row, j):
+        c = pl.ds(j * CHUNK, CHUNK)
+        r = pl.ds(row, K)
+        buf[pl.ds(K + row, K), c] = (k1[r, c].astype(F32) * v1[r, c].astype(F32)).astype(BF16)
+
+    loads[0].wait()
+    loads[1].wait()
+    for j in range(chunks):
+        product(T - K, j)
     peers = tp_n - 1
     for s in shifts:
         peers = peers + (d + s < n).astype(jnp.int32) + (d >= s).astype(jnp.int32)
     pl.semaphore_wait(barrier, peers)
-
-    def halo(j):
-        c = pl.ds(j * CHUNK, CHUNK)
-        return pltpu.make_async_remote_copy(
-            src_ref=buf.at[pl.ds(T, K), c], dst_ref=buf.at[pl.ds(0, K), c],
-            send_sem=halo_send.at[j], recv_sem=halo_recv.at[j],
-            device_id=(lax.rem(d + 1, n), t), device_id_type=MESH)
-
-    def product(row, j):
-        c = pl.ds(j * CHUNK, CHUNK)
-        r = pl.ds(row, K)
-        buf[pl.ds(K + row, K), c] = (k1[r, c].astype(F32) * v1[r, c].astype(F32)).astype(BF16)
-
-    loads[0].wait()
-    loads[1].wait()
-    for j in range(chunks):
-        product(T - K, j)
-
+    for j in range(chunks):
         @pl.when(d + 1 < n)
         def _(j=j):
             halo(j).start()
@@ -151,18 +150,23 @@
         root = lax.rsqrt(total * (1.0 / (C * tp_n)) + 1e-05)
         scale[...] = jnp.concatenate([root] * (K // 8), axis=0).T
 
-    def mode_rows(g, offset, sign):
-        sub = lax.broadcasted_iota(jnp.int32, (8, LANES), 0).astype(F32) * sign + offset
-        eight, first = [], []
+    def mode_tables(g, _):
+        c = lane(g)
+        sub = lax.broadcasted_iota(jnp.int32, (8, LANES), 0).astype(F32)
+        rate = rates[:, c]
+        eight_t[:, c] = jnp.exp(rate * -8.0)
+        weight_t[:, c] = residues[:, c] * jnp.sqrt(rate)
         for m in range(M):
-            rate = jnp.broadcast_to(rates[pl.ds(m, 1), lane(g)], (8, LANES))
-            eight.append(jnp.exp(rate * -8.0))
-            first.append(jnp.exp(-rate * sub))
-        return eight, first
-
-    def weight(g, m):
-        rate = rates[pl.ds(m, 1), lane(g)]
-        return residues[pl.ds(m, 1), lane(g)] * jnp.sqrt(rate)
+            row = jnp.broadcast_to(rates[pl.ds(m, 1), c], (8, LANES))
+            up_t[pl.ds(8 * m, 8), c] = jnp.exp(-row * sub)
+            down_t[pl.ds(8 * m, 8), c] = jnp.exp(-row * (7.0 - sub))
+        return 0
+
+    def eights(c):
+        return [jnp.broadcast_to(eight_t[pl.ds(m, 1), c], (8, LANES)) for m in range(M)]
+
+    def first_rows(factor, c):
+        return [up_t[pl.ds(8 * m, 8), c] * factor[pl.ds(m, 1), c] for m in range(M)]
 
     def tree_sum(terms):
         while len(terms) > 1:
@@ -177,7 +181,7 @@
 
     def normed(half, g, _):
         c = lane(g)
-        eight, first = mode_rows(g, 7.0, -1.0)
+        eight = eights(c)
         held = [jnp.zeros((8, LANES), F32)] * M
         for i in range(K // 16):
             r = pl.ds(half * K + i * 16, 16)
@@ -186,13 +190,9 @@
             wide = value.astype(F32)
             held = [h * a + wide[:8] for h, a in zip(held, eight)]
             held = [h * a + wide[8:] for h, a in zip(held, eight)]
+        into = low if half == 0 else state
         for m in range(M):
-            part = jnp.sum(held[m] * first[m], axis=0, keepdims=True)
-            row = pl.ds(m, 1)
-            if half == 0:
-                state[row, c] = state[row, c] + jnp.exp(rates[row, c] * -float(K)) * part
-            else:
-                state[row, c] = part
+            into[pl.ds(m, 1), c] = jnp.sum(held[m] * down_t[pl.ds(8 * m, 8), c], axis=0, keepdims=True)
         return 0
 
     def medium_spectrum(j, _):
@@ -206,13 +206,15 @@
     send_squares(1)
 
     def long_taps(g, _):
-        eight, first = mode_rows(g, 0.0, 1.0)
-        terms = [first[m] * weight(g, m) for m in range(M)]
+        c = lane(g)
+        eight = eights(c)
+        terms = first_rows(weight_t, c)
         for i in range(T // 16):
             rows, terms = next_rows(terms, eight)
-            hbuf[pl.ds(i * 16, 16), lane(g)] = rows.astype(BF16)
-        return 0
-
+            hbuf[pl.ds(i * 16, 16), c] = rows.astype(BF16)
+        return 0
+
+    lax.fori_loop(0, groups, mode_tables, 0)
     lax.fori_loop(0, groups, long_taps, 0)
     loads[7].wait()
     fl[...] = fl32[...].astype(BF16)
@@ -236,16 +238,34 @@
     rout_copy = pltpu.make_async_copy(rout, rout_h, out_sem.at[chunks])
     rout_copy.start()
     take_squares(0)
-    lax.fori_loop(0, groups, functools.partial(normed, 0), 0)
-    loads[9].wait()
-    gl[...] = gl32[...].astype(BF16)
-    loads[10].wait()
-
-    def hop(i):
+    per = groups // chunks
+
+    def hop(i, j):
+        c = pl.ds(j * CHUNK, CHUNK)
         return pltpu.make_async_remote_copy(
-            src_ref=st_send.at[i], dst_ref=st_recv.at[i],
-            send_sem=st_ssem.at[i], recv_sem=st_rsem.at[i],
+            src_ref=st_send.at[i, :, c], dst_ref=st_recv.at[i, :, c],
+            send_sem=st_ssem.at[i, j], recv_sem=st_rsem.at[i, j],
             device_id=(lax.rem(d + shifts[i], n), t), device_id_type=MESH)
+
+    def send_state(i, j):
+        @pl.when(d + shifts[i] < n)
+        def _():
+            c = pl.ds(j * CHUNK, CHUNK)
+            st_send[i, :, c] = state[:, c].astype(BF16)
+            hop(i, j).start()
+
+    def take_state(i, j):
+        s = shifts[i]
+
+        @pl.when(d >= s)
+        def _():
+            c = pl.ds(j * CHUNK, CHUNK)
+            hop(i, j).wait_recv()
+            arrived = st_recv[i, :, c].astype(F32)
+            rate = rates[:, c]
+            carry[:, c] += jnp.exp(rate * -float(T * (s - 1))) * arrived
+            if i + 1 < steps:
+                state[:, c] += jnp.exp(rate * -float(T * s)) * arrived
 
     def inside(j, _):
         c = cols(j)
@@ -253,44 +273,40 @@
         loc[:, c] = dot(gl[...], y) + skip2[:, c] * v2[:, c].astype(F32)
         return 0
 
-    carry[...] = jnp.zeros_like(carry)
-    done = 0
-    for i, s in enumerate(shifts):
-        st_send[i] = state[...].astype(BF16)
-
-        @pl.when(d + s < n)
-        def _(i=i):
-            hop(i).start()
-        upto = chunks * (i + 1) // steps
-        lax.fori_loop(done, upto, inside, 0)
-        done = upto
-
-        @pl.when(d >= s)
-        def _(i=i, s=s):
-            hop(i).wait_recv()
-            arrived = st_recv[i].astype(F32)
-            rate = rates[...]
-            carry[...] += jnp.exp(rate * -float(T * (s - 1))) * arrived
-            state[...] += jnp.exp(rate * -float(T * s)) * arrived
-
     def finish(g, _):
         c = lane(g)
-        eight, first = mode_rows(g, 1.0, 1.0)
-        terms = [first[m] * (weight(g, m) * carry[pl.ds(m, 1), c]) for m in range(M)]
+        eight = eights(c)
+        terms = first_rows(carry, c)
         for i in range(T // 16):
             r = pl.ds(i * 16, 16)
             rows, terms = next_rows(terms, eight)
             obuf[r, c] = (q2[r, c].astype(F32) * (loc[r, c] + rows)).astype(BF16)
         return 0
 
-    out_copies = []
-    per = groups // chunks
-    for j in range(chunks):
-        lax.fori_loop(j * per, (j + 1) * per, finish, 0)
-        c = pl.ds(j * CHUNK, CHUNK)
-        copy = pltpu.make_async_copy(obuf.at[:, c], lout_h.at[:, c], out_sem.at[j])
-        copy.start()
-        out_copies.append(copy)
+    carry[...] = jnp.zeros_like(carry)
+    for j in range(chunks):
+        lax.fori_loop(j * per, (j + 1) * per, functools.partial(normed, 0), 0)
+        c = pl.ds(j * CHUNK, CHUNK)
+        state[:, c] += jnp.exp(rates[:, c] * -float(K)) * low[:, c]
+        send_state(0, j)
+    loads[9].wait()
+    gl[...] = gl32[...].astype(BF16)
+    loads[10].wait()
+    done = 0
+    for i in range(steps):
+        for j in range(chunks):
+            take_state(i, j)
+            if i + 1 < steps:
+                send_state(i + 1, j)
+                continue
+            c = pl.ds(j * CHUNK, CHUNK)
+            carry[:, c] = carry[:, c] * weight_t[:, c] * jnp.exp(-rates[:, c])
+            lax.fori_loop(j * per, (j + 1) * per, finish, 0)
+            pltpu.make_async_copy(obuf.at[:, c], lout_h.at[:, c], out_sem.at[j]).start()
+        upto = chunks * (i + 1) // max(1, steps - 1)
+        if i + 1 < steps:
+            lax.fori_loop(done, upto, inside, 0)
+            done = upto
 
     for j in range(chunks):
         @pl.when(d + 1 < n)
@@ -299,10 +315,12 @@
     for i, s in enumerate(shifts):
         @pl.when(d + s < n)
         def _(i=i):
-            hop(i).wait_send()
+            for j in range(chunks):
+                hop(i, j).wait_send()
     rout_copy.wait()
-    for copy in out_copies:
-        copy.wait()
+    for j in range(chunks):
+        c = pl.ds(j * CHUNK, CHUNK)
+        pltpu.make_async_copy(obuf.at[:, c], lout_h.at[:, c], out_sem.at[j]).wait()
 
 
 def on_device(n, tp_n, q1, k1, v1, res, taps, skip1, gain, q2, k2, residues, rates, skip2):
@@ -340,6 +358,11 @@
             pltpu.VMEM((K, LANES), F32),
             pltpu.VMEM((M, C), F32),
             pltpu.VMEM((M, C), F32),
+            pltpu.VMEM((8 * M, C), F32),
+            pltpu.VMEM((8 * M, C), F32),
+            pltpu.VMEM((M, C), F32),
+            pltpu.VMEM((M, C), F32),
+            pltpu.VMEM((M, C), F32),
             pltpu.VMEM((steps, M, C), BF16),
             pltpu.VMEM((steps, M, C), BF16),
             pltpu.SemaphoreType.DMA((11,)),
@@ -348,8 +371,8 @@
             pltpu.SemaphoreType.DMA((chunks,)),
             pltpu.SemaphoreType.DMA((2, tp_n - 1)),
             pltpu.SemaphoreType.DMA((2, tp_n - 1)),
-            pltpu.SemaphoreType.DMA((steps,)),
-            pltpu.SemaphoreType.DMA((steps,)),
+            pltpu.SemaphoreType.DMA((steps, chunks)),
+            pltpu.SemaphoreType.DMA((steps, chunks)),
         ],
         compiler_params=pltpu.CompilerParams(
             collective_id=0, has_side_effects=True, vmem_limit_bytes=56 * 2**20),

time: 38.8 us -> 36.8 us (0.948)
  Pallas kernels: 34.6 us -> 32.6 us
    pallas_call x1, Pallas kernels: 34.6 us -> 32.6 us  [on_device(): pl.pallas_call(functools.partial(kernel, n, tp_n), out_shape=[jax.ShapeDt...]
where the time goes in v1:
time: 36.8 us; the launch traced here: 36.6 us
  Pallas kernels  32.6 us (89%)
  local copies, waits for them, and re-layouts  3.37 us (9%)
  between operations  0.65 us (2%)
    pallas_call x1, Pallas kernels, on_device(): pl.pallas_call(functools.partial(kernel, n, tp_n), out_shape=[jax.ShapeDt...  32.6 us
    unnamed x4, local copies, waits for them, and re-layouts  3.37 us

profile of v1, /device:TPU:20, one launch (start us, length us, event | category | flops | bytes accessed | tf_op | source)
XLA Modules:
  0.0 36.6 jit_solution(10708712669074402890)
XLA Ops:
  0.6 32.6 %shard_map.167 = (bf16[256,2048]{1,0:T(8,128)(2,1)}, bf16[256,2048]{1,0:T(8,128)(2,1)}) custom-call(bf16[256,2048]{1,0:T(8,128)(2,1)} %q1_h.1, bf16[256,2048]{1,0:T(8,128)(2,1)} %k1_h.1, bf16[256,2048]{1,0:T(8,128)(2,1)} %v1_h.1, bf16[256,2048]{1,0:T(8,128)(2,1)} %res_h.1, bf16[128,2048]{1,0:T(8,128)(2,1)} %taps_h.1, f32[1,2048]{1,0:T(1,128)} %bitcast.3, ...), custom_call_target="tpu_custom_call" | custom-call | flops 2539520000 | bytes 10485760 | tf_op jit(solution)/shard_map/pallas_call | solution.py:338
  33.3 0.0 copy-start
  33.3 2.4 %copy.20 = bf16[256,2048]{1,0:T(8,128)(2,1)} copy(bf16[256,2048]{1,0:T(8,128)(2,1)} %get-tuple-element.4) | data formatting | bytes 2097152
  35.7 0.0 copy-done
  35.7 1.0 %copy.21 = bf16[256,2048]{1,0:T(8,128)(2,1)} copy(bf16[256,2048]{1,0:T(8,128)(2,1)S(1)} %copy-done) | data formatting | bytes 2097152
Async XLA Ops:
  33.3 2.4 %copy-start = (bf16[256,2048]{1,0:T(8,128)(2,1)S(1)}, bf16[256,2048]{1,0:T(8,128)(2,1)}, u32[]{:S(2)}) copy-start(bf16[256,2048]{1,0:T(8,128)(2,1)} %get-tuple-element.5) | copy-start | bytes 3145732

commit v2 on v1

--- a/solution.py
+++ b/solution.py
@@ -36,10 +36,10 @@
 
 def kernel(
     n, tp_n,
-    q1_h, k1_h, v1_h, res_h, taps_h, skip1, gain, q2_h, k2_h, residues, rates, skip2,
+    q1_h, k1_h, v1_h, res_h, taps_h, skip1_h, gain_h, q2_h, k2_h, residues_h, rates_h, skip2_h,
     fm_h, gm_h, fl_h, gl_h,
     rout_h, lout_h,
-    q1, k1, v1, res, taps, q2, k2, fm32, gm32, fl32, gl32, fm, gm, fl, gl,
+    q1, k1, v1, res, taps, skip1, gain, q2, k2, residues, rates, skip2, fm32, gm32, fl32, gl32, fm, gm, fl, gl,
     buf, spec_m, spec_l, hbuf, rout, v2, loc, obuf,
     sq_acc, sq_send, sq_recv, scale, eight_t, weight_t, up_t, down_t, low, state, carry, st_send, st_recv,
     in_sem, out_sem, halo_send, halo_recv, sq_ssem, sq_rsem, st_ssem, st_rsem,
@@ -57,15 +57,18 @@
         return pl.ds(pl.multiple_of(g * LANES, LANES), LANES)
 
     def cols(j):
-        return pl.ds(pl.multiple_of(j * CHUNK, CHUNK), CHUNK)
-
+        return pl.ds(j * CHUNK, CHUNK)
+
+    last, top = pl.ds(T - K, K), pl.ds(0, T - K)
     pairs = [
-        (k1_h, k1), (v1_h, v1), (fm_h, fm32), (taps_h, taps), (gm_h, gm32), (q1_h, q1), (res_h, res),
-        (fl_h, fl32), (k2_h, k2), (gl_h, gl32), (q2_h, q2),
+        (k1_h.at[last], k1.at[last]), (v1_h.at[last], v1.at[last]),
+        (rates_h, rates), (residues_h, residues), (k1_h.at[top], k1.at[top]), (v1_h.at[top], v1.at[top]),
+        (fm_h, fm32), (taps_h, taps), (gm_h, gm32), (skip1_h, skip1), (q1_h, q1), (res_h, res),
+        (k2_h, k2), (gain_h, gain), (fl_h, fl32), (gl_h, gl32), (skip2_h, skip2), (q2_h, q2),
     ]
     loads = [pltpu.make_async_copy(a, b, in_sem.at[i]) for i, (a, b) in enumerate(pairs)]
-    for load in loads:
-        load.start()
+    loads[0].start()
+    loads[1].start()
 
     barrier = pltpu.get_barrier_semaphore()
     shifts = [1 << i for i in range(steps)]
@@ -80,19 +83,21 @@
     for o in range(1, tp_n):
         pl.semaphore_signal(barrier, inc=1, device_id=(d, lax.rem(t + o, tp_n)), device_id_type=MESH)
     def halo(j):
-        c = pl.ds(j * CHUNK, CHUNK)
+        c = cols(j)
         return pltpu.make_async_remote_copy(
             src_ref=buf.at[pl.ds(T, K), c], dst_ref=buf.at[pl.ds(0, K), c],
             send_sem=halo_send.at[j], recv_sem=halo_recv.at[j],
             device_id=(lax.rem(d + 1, n), t), device_id_type=MESH)
 
     def product(row, j):
-        c = pl.ds(j * CHUNK, CHUNK)
+        c = cols(j)
         r = pl.ds(row, K)
         buf[pl.ds(K + row, K), c] = (k1[r, c].astype(F32) * v1[r, c].astype(F32)).astype(BF16)
 
     loads[0].wait()
     loads[1].wait()
+    for load in loads[2:]:
+        load.start()
     for j in range(chunks):
         product(T - K, j)
     peers = tp_n - 1
@@ -103,18 +108,6 @@
         @pl.when(d + 1 < n)
         def _(j=j):
             halo(j).start()
-    for j in range(chunks):
-        product(0, j)
-
-    @pl.when(d == 0)
-    def _():
-        buf[pl.ds(0, K), :] = jnp.zeros((K, C), BF16)
-
-    for i in range(2, 7):
-        loads[i].wait()
-    fm[...] = fm32[...].astype(BF16)
-    gm[...] = gm32[...].astype(BF16)
-
     def medium(row, j):
         c = cols(j)
         r = pl.ds(row, K)
@@ -195,16 +188,6 @@
             into[pl.ds(m, 1), c] = jnp.sum(held[m] * down_t[pl.ds(8 * m, 8), c], axis=0, keepdims=True)
         return 0
 
-    def medium_spectrum(j, _):
-        c = cols(j)
-        spec_m[:, c] = dot(fm[:, :K], taps[:, c])
-        medium(K, j)
-        return 0
-
-    sq_acc[...] = jnp.zeros_like(sq_acc)
-    lax.fori_loop(0, chunks, medium_spectrum, 0)
-    send_squares(1)
-
     def long_taps(g, _):
         c = lane(g)
         eight = eights(c)
@@ -214,17 +197,33 @@
             hbuf[pl.ds(i * 16, 16), c] = rows.astype(BF16)
         return 0
 
+    def long_spectrum(j):
+        spec_l[:, cols(j)] = dot(fl[...], hbuf[:, cols(j)])
+
+    loads[2].wait()
+    loads[3].wait()
     lax.fori_loop(0, groups, mode_tables, 0)
+
+    @pl.when(d == 0)
+    def _():
+        buf[pl.ds(0, K), :] = jnp.zeros((K, C), BF16)
+
+    for i in range(4, 12):
+        loads[i].wait()
+    fm[...] = fm32[...].astype(BF16)
+    gm[...] = gm32[...].astype(BF16)
+    for j in range(chunks):
+        product(0, j)
+    sq_acc[...] = jnp.zeros_like(sq_acc)
+    for j in range(chunks):
+        spec_m[:, cols(j)] = dot(fm[:, :K], taps[:, cols(j)])
+        medium(K, j)
+    send_squares(1)
     lax.fori_loop(0, groups, long_taps, 0)
-    loads[7].wait()
+    for i in range(12, 18):
+        loads[i].wait()
     fl[...] = fl32[...].astype(BF16)
-
-    def long_spectrum(j, _):
-        spec_l[:, cols(j)] = dot(fl[...], hbuf[:, cols(j)])
-        return 0
-
-    lax.fori_loop(0, chunks, long_spectrum, 0)
-    loads[8].wait()
+    gl[...] = gl32[...].astype(BF16)
     take_squares(1)
     lax.fori_loop(0, groups, functools.partial(normed, 1), 0)
 
@@ -237,11 +236,14 @@
     send_squares(0)
     rout_copy = pltpu.make_async_copy(rout, rout_h, out_sem.at[chunks])
     rout_copy.start()
+    for j in range(chunks):
+        long_spectrum(j)
     take_squares(0)
+
     per = groups // chunks
 
     def hop(i, j):
-        c = pl.ds(j * CHUNK, CHUNK)
+        c = cols(j)
         return pltpu.make_async_remote_copy(
             src_ref=st_send.at[i, :, c], dst_ref=st_recv.at[i, :, c],
             send_sem=st_ssem.at[i, j], recv_sem=st_rsem.at[i, j],
@@ -250,7 +252,7 @@
     def send_state(i, j):
         @pl.when(d + shifts[i] < n)
         def _():
-            c = pl.ds(j * CHUNK, CHUNK)
+            c = cols(j)
             st_send[i, :, c] = state[:, c].astype(BF16)
             hop(i, j).start()
 
@@ -259,7 +261,7 @@
 
         @pl.when(d >= s)
         def _():
-            c = pl.ds(j * CHUNK, CHUNK)
+            c = cols(j)
             hop(i, j).wait_recv()
             arrived = st_recv[i, :, c].astype(F32)
             rate = rates[:, c]
@@ -267,11 +269,10 @@
             if i + 1 < steps:
                 state[:, c] += jnp.exp(rate * -float(T * s)) * arrived
 
-    def inside(j, _):
+    def inside(j):
         c = cols(j)
         y = complex_product(dot(fl[...], v2[:, c]), spec_l[:, c])
         loc[:, c] = dot(gl[...], y) + skip2[:, c] * v2[:, c].astype(F32)
-        return 0
 
     def finish(g, _):
         c = lane(g)
@@ -286,27 +287,24 @@
     carry[...] = jnp.zeros_like(carry)
     for j in range(chunks):
         lax.fori_loop(j * per, (j + 1) * per, functools.partial(normed, 0), 0)
-        c = pl.ds(j * CHUNK, CHUNK)
+        c = cols(j)
         state[:, c] += jnp.exp(rates[:, c] * -float(K)) * low[:, c]
         send_state(0, j)
-    loads[9].wait()
-    gl[...] = gl32[...].astype(BF16)
-    loads[10].wait()
-    done = 0
-    for i in range(steps):
+    waiting = list(range(chunks))
+    for i in range(steps - 1):
         for j in range(chunks):
+            if j % 2 == 0 and waiting:
+                inside(waiting.pop(0))
             take_state(i, j)
-            if i + 1 < steps:
-                send_state(i + 1, j)
-                continue
-            c = pl.ds(j * CHUNK, CHUNK)
-            carry[:, c] = carry[:, c] * weight_t[:, c] * jnp.exp(-rates[:, c])
-            lax.fori_loop(j * per, (j + 1) * per, finish, 0)
-            pltpu.make_async_copy(obuf.at[:, c], lout_h.at[:, c], out_sem.at[j]).start()
-        upto = chunks * (i + 1) // max(1, steps - 1)
-        if i + 1 < steps:
-            lax.fori_loop(done, upto, inside, 0)
-            done = upto
+            send_state(i + 1, j)
+    for j in waiting:
+        inside(j)
+    for j in range(chunks):
+        c = cols(j)
+        take_state(steps - 1, j)
+        carry[:, c] = carry[:, c] * weight_t[:, c] * jnp.exp(-rates[:, c])
+        lax.fori_loop(j * per, (j + 1) * per, finish, 0)
+        pltpu.make_async_copy(obuf.at[:, c], lout_h.at[:, c], out_sem.at[j]).start()
 
     for j in range(chunks):
         @pl.when(d + 1 < n)
@@ -319,7 +317,7 @@
                 hop(i, j).wait_send()
     rout_copy.wait()
     for j in range(chunks):
-        c = pl.ds(j * CHUNK, CHUNK)
+        c = cols(j)
         pltpu.make_async_copy(obuf.at[:, c], lout_h.at[:, c], out_sem.at[j]).wait()
 
 
@@ -333,15 +331,17 @@
     fm, gm = half_bin_tables(2 * K, 2 * K, K, 2 * K)
     fl, gl = half_bin_tables(2 * T, T, 0, T)
     hbm = pl.BlockSpec(memory_space=pl.ANY)
-    vmem = pl.BlockSpec(memory_space=pltpu.VMEM)
+    line = pltpu.VMEM((1, C), F32)
+    modes = pltpu.VMEM((M, C), F32)
     wide = pltpu.VMEM((T, C), BF16)
     return pl.pallas_call(
         functools.partial(kernel, n, tp_n),
         out_shape=[jax.ShapeDtypeStruct((T, C), BF16)] * 2,
-        in_specs=[hbm] * 5 + [vmem] * 2 + [hbm] * 2 + [vmem] * 3 + [hbm] * 4,
+        in_specs=[hbm] * 16,
         out_specs=[hbm] * 2,
         scratch_shapes=[
-            wide, wide, wide, wide, pltpu.VMEM((K, C), BF16), wide, wide,
+            wide, wide, wide, wide, pltpu.VMEM((K, C), BF16), line, line, wide, wide,
+            modes, modes, line,
             pltpu.VMEM(fm.shape, F32), pltpu.VMEM(gm.shape, F32),
             pltpu.VMEM(fl.shape, F32), pltpu.VMEM(gl.shape, F32),
             pltpu.VMEM(fm.shape, BF16), pltpu.VMEM(gm.shape, BF16),
@@ -356,16 +356,16 @@
             pltpu.VMEM((2, 8, K), F32),
             pltpu.VMEM((2, tp_n - 1, 8, K), F32),
             pltpu.VMEM((K, LANES), F32),
-            pltpu.VMEM((M, C), F32),
-            pltpu.VMEM((M, C), F32),
+            modes,
+            modes,
             pltpu.VMEM((8 * M, C), F32),
             pltpu.VMEM((8 * M, C), F32),
-            pltpu.VMEM((M, C), F32),
-            pltpu.VMEM((M, C), F32),
-            pltpu.VMEM((M, C), F32),
+            modes,
+            modes,
+            modes,
             pltpu.VMEM((steps, M, C), BF16),
             pltpu.VMEM((steps, M, C), BF16),
-            pltpu.SemaphoreType.DMA((11,)),
+            pltpu.SemaphoreType.DMA((18,)),
             pltpu.SemaphoreType.DMA((chunks + 1,)),
             pltpu.SemaphoreType.DMA((chunks,)),
             pltpu.SemaphoreType.DMA((chunks,)),

time: 36.8 us -> 35.2 us (0.957)
  Pallas kernels: 32.6 us -> 30.8 us
    pallas_call x1, Pallas kernels: 32.6 us -> 30.8 us  [on_device(): pl.pallas_call(functools.partial(kernel, n, tp_n), out_shape=[jax.ShapeDt...]
where the time goes in v2:
time: 35.2 us; the launch traced here: 34.8 us
  Pallas kernels  30.8 us (88%)
  local copies, waits for them, and re-layouts  3.37 us (10%)
  between operations  0.65 us (2%)
    pallas_call x1, Pallas kernels, on_device(): pl.pallas_call(functools.partial(kernel, n, tp_n), out_shape=[jax.ShapeDt...  30.8 us
    unnamed x4, local copies, waits for them, and re-layouts  3.37 us

profile of v2, /device:TPU:20, one launch (start us, length us, event | category | flops | bytes accessed | tf_op | source)
XLA Modules:
  0.0 34.8 jit_solution(937646350703629710)
XLA Ops:
  0.6 30.8 %shard_map.167 = (bf16[256,2048]{1,0:T(8,128)(2,1)}, bf16[256,2048]{1,0:T(8,128)(2,1)}) custom-call(bf16[256,2048]{1,0:T(8,128)(2,1)} %q1_h.1, bf16[256,2048]{1,0:T(8,128)(2,1)} %k1_h.1, bf16[256,2048]{1,0:T(8,128)(2,1)} %v1_h.1, bf16[256,2048]{1,0:T(8,128)(2,1)} %res_h.1, bf16[128,2048]{1,0:T(8,128)(2,1)} %taps_h.1, f32[1,2048]{1,0:T(1,128)} %bitcast.3, ...), custom_call_target="tpu_custom_call" | custom-call | flops 2539520000 | bytes 10485760 | tf_op jit(solution)/shard_map/pallas_call | solution.py:337
  31.4 0.0 copy-start
  31.5 2.4 %copy.20 = bf16[256,2048]{1,0:T(8,128)(2,1)} copy(bf16[256,2048]{1,0:T(8,128)(2,1)} %get-tuple-element.4) | data formatting | bytes 2097152
  33.8 0.0 copy-done
  33.8 1.0 %copy.21 = bf16[256,2048]{1,0:T(8,128)(2,1)} copy(bf16[256,2048]{1,0:T(8,128)(2,1)S(1)} %copy-done) | data formatting | bytes 2097152
Async XLA Ops:
  31.4 2.4 %copy-start = (bf16[256,2048]{1,0:T(8,128)(2,1)S(1)}, bf16[256,2048]{1,0:T(8,128)(2,1)}, u32[]{:S(2)}) copy-start(bf16[256,2048]{1,0:T(8,128)(2,1)} %get-tuple-element.5) | copy-start | bytes 3145732
